TPU v7x, 256 devices: a whole 4x4x8 slice. The times are simulated.
256 devices in a mesh: frame: 8 (over y_lo, x), row: 32 (over y_hi, z, core).
Axes of the slice: x: 4, y: 4 (y_hi: 2, y_lo: 2; y = y_hi * 2 + y_lo), z: 8, core: 2. Of those that a mesh axis runs over, the one named last changes fastest.
Arguments:
- latent: float32 [16, 64, 320, 128], P('frame', 'row'), may hold values from -51 to 51
- cotangent: float32 [16, 64, 320, 128], P('frame', 'row'), may hold values from -6 to 6
- gn_gain: float32 [320], replicated, may hold values from 0.1 to 1.9
- gn_bias: float32 [320], replicated, may hold values from -3 to 3
- w_spatial: float32 [3, 3, 320, 320], replicated, may hold values from -0.109375 to 0.109375
- w_temporal: float32 [3, 320, 320], replicated, may hold values from -0.1875 to 0.1875
- ln_gain: float32 [320], replicated, may hold values from 0.1 to 1.9
- ln_bias: float32 [320], replicated, may hold values from -3 to 3
- w_query: float32 [320, 320], replicated, may hold values from -1.5 to 1.5
- w_key: float32 [320, 320], replicated, may hold values from -1.5 to 1.5
- w_value: float32 [320, 320], replicated, may hold values from -0.3125 to 0.3125
- w_out: float32 [320, 320], replicated, may hold values from -0.3125 to 0.3125
Outputs:
- output: float32 [16, 64, 320, 128], P('frame', 'row')
- grad_latent: float32 [16, 64, 320, 128], P('frame', 'row')
All inputs are finite; a program needn't handle non-finite values.
Results may differ from a plain program's by a relative error of at most 0.0003.
Values sent between devices are 32-bit elements; how exact they have to be, the bound alone decides.
A program may use at most 128 MiB of HBM per device.

v0:
```python
import functools

import jax
import jax.numpy as jnp
from jax import lax
from jax.experimental import pallas as pl
from jax.experimental.pallas import tpu as pltpu
from jax.sharding import PartitionSpec as P

C = 320
GROUPS = 32
PER_GROUP = C // GROUPS
HEADS = 5
HEAD_DIM = 64
EPSILON = 1e-05
LANES = 128
KDIM = 1024
QUARTER = C // 4
F32 = jnp.float32
BF16 = jnp.bfloat16
HIGHEST = lax.Precision.HIGHEST
MESH = pl.DeviceIdType.MESH
NT = (((1,), (1,)), ((), ()))

LAT, COT, SPA, GSP, GHI, OUT = 0, 2, 4, 6, 8, 10


def iota(shape, dim):
    return lax.broadcasted_iota(jnp.int32, shape, dim)


def roll(x, shift):
    shift = shift % x.shape[1]
    return x if shift == 0 else pltpu.roll(x, shift, 1)


def dot(a, b):
    return jnp.dot(a, b, preferred_element_type=F32)


def dot_nt(a, b):
    return lax.dot_general(a, b, NT, preferred_element_type=F32)


def exact_nt(a, b):
    return lax.dot_general(a, b, NT, precision=HIGHEST, preferred_element_type=F32)


def split(x):
    hi = x.astype(BF16)
    lo = (x - hi.astype(F32)).astype(BF16)
    return hi, lo


def transpose_chunks(xs):
    lane = iota(xs[0].shape, 1)
    bits = [(lane & (16 << i)) != 0 for i in range(3)]
    ys = [roll(x, 16 * m) for m, x in enumerate(xs)]
    out = []
    for j in range(8):
        level = [ys[(p - j) % 8] for p in range(8)]
        for bit in bits:
            level = [
                jnp.where(bit, level[2 * i + 1], level[2 * i]) for i in range(len(level) // 2)
            ]
        out.append(roll(level[0], -16 * j))
    return out


def interleave(x0, x1):
    low = (iota(x0.shape, 1) & 8) == 0
    return jnp.where(low, x0, roll(x1, 8)), jnp.where(low, roll(x0, -8), x1)


def put3(ref, base, lanes, x):
    hi, lo = split(x)
    ref[pl.ds(base, 256), lanes] = hi[:256]
    ref[pl.ds(base + 256, 256), lanes] = lo[:256]
    ref[pl.ds(base + 512, 256), lanes] = hi[:256]
    ref[pl.ds(base + 768, 64), lanes] = hi[256:]
    ref[pl.ds(base + 832, 64), lanes] = lo[256:]
    ref[pl.ds(base + 896, 64), lanes] = hi[256:]


def prepare(w, ref):
    hi = w.astype(BF16).astype(F32)
    lo = w - hi
    ref[:, 0:256] = hi[:, :256].astype(BF16)
    ref[:, 256:512] = hi[:, :256].astype(BF16)
    ref[:, 512:768] = lo[:, :256].astype(BF16)
    ref[:, 768:896] = jnp.concatenate([hi[:, 256:], hi[:, 256:]], axis=1).astype(BF16)
    ref[:, 896:1024] = jnp.concatenate([lo[:, 256:], jnp.zeros((C, 64), F32)], axis=1).astype(BF16)


def kernel(
    n_frame,
    n_row,
    latent,
    cotangent,
    vecs,
    w_spatial,
    w_temporal,
    w_query,
    w_key,
    w_value,
    w_out,
    output,
    grad_latent,
    lat4,
    cot_own,
    gs4,
    hat_s,
    fac_s,
    ghid,
    gact,
    wsp,
    wte,
    wat,
    lsp,
    lte_f,
    lte_b,
    lqkv,
    lat_b,
    lout_f,
    rhs9,
    rhs3,
    rhs1,
    sbuf,
    rbuf,
    stat_s,
    stat_r,
    bcast,
    lcol,
    scol,
    qkv,
    gcol,
    acol,
    hcol,
    dqkv,
    load_sem,
    ssem,
    rsem,
    halo_s,
    halo_r,
    stat_ss,
    stat_rs,
):
    fi = lax.axis_index("frame")
    ri = lax.axis_index("row")
    members = 2 * n_row * PER_GROUP * LANES
    has_low = ri > 0
    has_high = ri < n_row - 1

    loads = []
    for r in range(2):
        for f in range(2):
            loads.append((latent.at[f, r], lat4.at[1 + r, f]))
    for r in range(2):
        for f in range(2):
            loads.append((cotangent.at[f, r], cot_own.at[r, f]))
    loads.append((w_spatial, wsp))
    loads.append((w_temporal, wte))
    for i, w in enumerate((w_query, w_key, w_value, w_out)):
        loads.append((w, wat.at[i]))
    copies = [
        pltpu.make_async_copy(src, dst, load_sem.at[i]) for i, (src, dst) in enumerate(loads)
    ]
    for c in copies:
        c.start()

    barrier = pltpu.get_barrier_semaphore()

    @pl.loop(1, n_row)
    def _(k):
        pl.semaphore_signal(
            barrier, inc=1, device_id={"row": lax.rem(ri + k, n_row)}, device_id_type=MESH
        )

    @pl.loop(1, n_frame)
    def _(k):
        pl.semaphore_signal(
            barrier, inc=1, device_id={"frame": lax.rem(fi + k, n_frame)}, device_id_type=MESH
        )

    def a2a_send(t):
        @pl.loop(1, n_frame)
        def _(k):
            dest = lax.rem(fi + k, n_frame)
            pltpu.make_async_remote_copy(
                src_ref=sbuf.at[t, dest],
                dst_ref=rbuf.at[t, fi],
                send_sem=ssem.at[t],
                recv_sem=rsem.at[t],
                device_id={"frame": dest},
                device_id_type=MESH,
            ).start()

        rbuf[t, fi] = sbuf[t, fi]

    def bytes_wait(ref, sem):
        pltpu.make_async_copy(ref, ref, sem).wait()

    def a2a_wait(t):
        bytes_wait(rbuf.at[t, pl.ds(0, n_frame - 1)], rsem.at[t])

    def pack_frame(src, t):
        @pl.loop(0, 5)
        def _(i):
            xs = []
            for q in range(4):
                start = pl.multiple_of(q * QUARTER + i * 16, 16)
                xs.extend(interleave(src(0, start), src(1, start)))
            for j, x in enumerate(transpose_chunks(xs)):
                sbuf[t, j, pl.ds(pl.multiple_of(i * 16, 16), 16), :] = x

    def unpack_frame(t, store):
        @pl.loop(0, 5)
        def _(i):
            at = pl.ds(pl.multiple_of(i * 16, 16), 16)
            ys = transpose_chunks([rbuf[t, j, at, :] for j in range(8)])
            for q in range(4):
                x0, x1 = interleave(ys[2 * q], ys[2 * q + 1])
                start = pl.multiple_of(q * QUARTER + i * 16, 16)
                store(0, start, x0)
                store(1, start, x1)

    def pack_col(src, t):
        @pl.loop(0, 5)
        def _(i):
            xs = []
            for q in range(4):
                start = pl.multiple_of(q * QUARTER + i * 16, 16)
                for h in range(2):
                    xs.append(src[pl.ds(start, 16), h * LANES : (h + 1) * LANES])
            for s, x in enumerate(transpose_chunks(xs)):
                sbuf[t, s, pl.ds(pl.multiple_of(i * 16, 16), 16), :] = x

    def unpack_col(t, dst):
        @pl.loop(0, 5)
        def _(i):
            at = pl.ds(pl.multiple_of(i * 16, 16), 16)
            ys = transpose_chunks([rbuf[t, s, at, :] for s in range(8)])
            for q in range(4):
                start = pl.multiple_of(q * QUARTER + i * 16, 16)
                for h in range(2):
                    dst[pl.ds(start, 16), h * LANES : (h + 1) * LANES] = ys[2 * q + h]

    chan = iota((C, LANES), 0)
    group = iota((C, LANES), 1)
    member = ((chan >= group * PER_GROUP) & (chan < group * PER_GROUP + PER_GROUP)).astype(F32)

    def pack_stats(which, parts):
        total = jnp.zeros((8, C), F32)
        at = iota((8, LANES), 0)
        for k, part in enumerate(parts):
            total = total + exact_nt((at == k).astype(F32), part)
        tile = jnp.dot(total, member, precision=HIGHEST, preferred_element_type=F32)
        stat_s[which] = tile
        stat_r[which, ri] = tile

    def send_stats(which):
        @pl.loop(1, n_row)
        def _(k):
            pltpu.make_async_remote_copy(
                src_ref=stat_s.at[which],
                dst_ref=stat_r.at[which, ri],
                send_sem=stat_ss.at[which],
                recv_sem=stat_rs.at[which],
                device_id={"row": lax.rem(ri + k, n_row)},
                device_id_type=MESH,
            ).start()

    def total_stats(which):
        bytes_wait(stat_r.at[which, pl.ds(0, n_row - 1)], stat_rs.at[which])
        return jnp.sum(stat_r[which], axis=0) * (1.0 / members)

    def spread(rows, at):
        cols = exact_nt(member, rows)
        for k in range(4):
            bcast[at + k] = jnp.broadcast_to(cols[:, k : k + 1], (C, LANES))

    def halo_copies(buf, which):
        up = pltpu.make_async_remote_copy(
            src_ref=buf.at[2],
            dst_ref=buf.at[0],
            send_sem=halo_s.at[which],
            recv_sem=halo_r.at[which],
            device_id={"row": lax.rem(ri + 1, n_row)},
            device_id_type=MESH,
        )
        down = pltpu.make_async_remote_copy(
            src_ref=buf.at[1],
            dst_ref=buf.at[3],
            send_sem=halo_s.at[which + 1],
            recv_sem=halo_r.at[which + 1],
            device_id={"row": lax.rem(ri + n_row - 1, n_row)},
            device_id_type=MESH,
        )
        return up, down

    for c in copies[:4]:
        c.wait()
    parts = []
    for f in range(2):
        a, b = lat4[1, f], lat4[2, f]
        parts.append(a + b)
    for f in range(2):
        a, b = lat4[1, f], lat4[2, f]
        parts.append(a * a + b * b)
    pack_stats(0, parts)
    for r in range(2):
        pack_frame(lambda f, start: lat4[1 + r, f, pl.ds(start, 16), :], LAT + r)
    for c in copies[4:8]:
        c.wait()
    for r in range(2):
        pack_frame(lambda f, start: cot_own[r, f, pl.ds(start, 16), :], COT + r)

    pl.semaphore_wait(barrier, n_row - 1 + n_frame - 1)
    send_stats(0)
    lat_up, lat_down = halo_copies(lat4, 0)
    lat_up.start()
    lat_down.start()
    a2a_send(LAT)
    a2a_send(COT)

    for c in copies[8:]:
        c.wait()

    @pl.loop(0, 9)
    def _(t):
        prepare(wsp[t].T, lsp.at[t])

    @pl.loop(0, 3)
    def _(t):
        prepare(wte[t].T, lte_f.at[t])

    @pl.loop(0, 12)
    def _(t):
        rhs9[pl.ds(pl.multiple_of(t * KDIM + 960, 64), 64), :] = jnp.zeros((64, 256), BF16)

    for t in range(3):
        rhs3[t, pl.ds(960, 64), :] = jnp.zeros((64, 256), BF16)
    rhs1[pl.ds(960, 64), :] = jnp.zeros((64, 256), BF16)

    eye = (iota((C, C), 0) == iota((C, C), 1)).astype(F32)
    cols = exact_nt(eye, vecs[...])
    for k in range(4):
        bcast[4 + k] = jnp.broadcast_to(cols[:, k : k + 1], (C, LANES))

    mean2 = total_stats(0)
    at8 = iota((8, LANES), 0)
    var = pltpu.roll(mean2, 6, 0) - mean2 * mean2
    rstd = lax.rsqrt(jnp.where(at8 < 2, var, 1.0) + EPSILON)
    spread(jnp.where(at8 < 2, mean2, pltpu.roll(rstd, 2, 0)), 0)

    lat_up.wait_recv()
    lat_down.wait_recv()

    lane = iota((C, LANES), 1)

    def shifted_rhs(r4, f, x):
        for b in range(3):
            if b == 0:
                y = jnp.where(lane == 0, 0.0, roll(x, 1))
            elif b == 1:
                y = x
            else:
                y = jnp.where(lane == LANES - 1, 0.0, roll(x, LANES - 1))
            base = pl.multiple_of((r4 * 3 + b) * KDIM, KDIM)
            put3(rhs9, base, pl.ds(f * LANES, LANES), y)

    def inside(r4):
        return ((r4 > 0) | has_low) & ((r4 < 3) | has_high)

    @pl.loop(0, 4)
    def _(r4):
        for f in range(2):
            hat = (lat4[r4, f] - bcast[f]) * bcast[2 + f]
            shifted = hat * bcast[4] + bcast[5]
            sigma = 1.0 / (1.0 + jnp.exp(-shifted))
            act = shifted * sigma
            hat_s[r4, f] = hat
            fac_s[r4, f] = sigma * (1.0 + shifted * (1.0 - sigma)) * bcast[4]
            shifted_rhs(r4, f, jnp.where(inside(r4), act, 0.0))

    def conv(rows, taps, base):
        total = None
        for t in taps:
            start = pl.multiple_of(base + (t - taps[0]) * KDIM, KDIM)
            term = dot(lsp[t], rhs9[pl.ds(start, KDIM), :])
            total = term if total is None else total + term
        return total

    @pl.loop(0, 2)
    def _(r):
        scol[...] = conv(r, list(range(9)), r * (3 * KDIM))
        pack_frame(
            lambda f, start: scol[pl.ds(start, 16), f * LANES : (f + 1) * LANES], SPA + r
        )
        a2a_send(SPA + r)

        @pl.when(r == 0)
        def _():
            a2a_send(LAT + 1)

    a2a_send(COT + 1)

    for i in range(3):
        prepare(wat[i].T, lqkv.at[pl.ds(i * C, C)])
    for i in range(4):
        prepare(wat[i], lat_b.at[i])
    prepare(wat[3].T, lout_f)
    for k in range(3):
        prepare(wte[2 - k], lte_b.at[k])

    half = LANES
    same = (iota((half, half), 0) & 7) == (iota((half, half), 1) & 7)
    scale = HEAD_DIM ** (-0.5)

    def temporal(x, h):
        lanes = pl.ds(h * half, half)
        put3(rhs3.at[0], 0, lanes, jnp.where(lane < 8, 0.0, roll(x, 8)))
        put3(rhs3.at[1], 0, lanes, x)
        put3(rhs3.at[2], 0, lanes, jnp.where(lane >= half - 8, 0.0, roll(x, half - 8)))

    def temporal_mix(weights):
        return (
            dot(weights[0], rhs3[0]) + dot(weights[1], rhs3[1]) + dot(weights[2], rhs3[2])
        )

    def twice(k):
        return jnp.concatenate([bcast[k], bcast[k]], axis=1)

    def stack3(x, axis):
        hi, lo = split(x)
        return jnp.concatenate([hi, lo, hi], axis=axis)

    def weigh3(x, axis):
        hi, lo = split(x)
        return jnp.concatenate([hi, hi, lo], axis=axis)

    def turned(x):
        hi = x.astype(BF16).astype(F32)
        lo = x - hi
        return jnp.concatenate([hi, hi, lo], axis=0).T.astype(BF16)

    @pl.loop(0, 2)
    def _(r):
        a2a_wait(LAT + r)
        unpack_col(LAT + r, lcol)
        a2a_wait(SPA + r)
        unpack_col(SPA + r, scol)
        for h in range(2):
            temporal(scol[:, h * half : (h + 1) * half], h)
        hidden = lcol[...] + temporal_mix(lte_f)
        hcol[r] = hidden
        centered = hidden - jnp.sum(hidden, axis=0, keepdims=True) * (1.0 / C)
        spread_ = jnp.sum(centered * centered, axis=0, keepdims=True) * (1.0 / C)
        ln_rstd = lax.rsqrt(spread_ + EPSILON)
        normal = centered * ln_rstd
        lcol[...] = normal
        normed = normal * twice(6) + twice(7)
        for h in range(2):
            put3(rhs1, 0, pl.ds(h * half, half), normed[:, h * half : (h + 1) * half])
        qkv[...] = dot(lqkv[...], rhs1[...])

        a2a_wait(COT + r)
        unpack_col(COT + r, gcol)
        for h in range(2):
            put3(rhs1, 0, pl.ds(h * half, half), gcol[:, h * half : (h + 1) * half])
        scol[...] = dot(lat_b[3], rhs1[...])

        for head in range(HEADS):
            for h in range(2):
                rows = slice(head * HEAD_DIM, (head + 1) * HEAD_DIM)
                lanes = slice(h * half, (h + 1) * half)
                q = qkv[rows, lanes]
                k = qkv[C + head * HEAD_DIM : C + (head + 1) * HEAD_DIM, lanes]
                v = qkv[2 * C + head * HEAD_DIM : 2 * C + (head + 1) * HEAD_DIM, lanes]
                g = scol[rows, lanes]
                scores = jnp.where(same, dot(turned(k), stack3(q, 0)) * scale, -1e30)
                e = jnp.exp(scores - jnp.max(scores, axis=0, keepdims=True))
                p = e * (1.0 / jnp.sum(e, axis=0, keepdims=True))
                p3 = stack3(p, 0)
                acol[r, rows, lanes] = dot(weigh3(v, 1), p3)
                gp = dot(turned(v), stack3(g, 0))
                gs = p * (gp - jnp.sum(p * gp, axis=0, keepdims=True)) * scale
                dqkv[0, rows, lanes] = dot(weigh3(k, 1), stack3(gs, 0))
                dqkv[1, rows, lanes] = dot_nt(weigh3(q, 1), stack3(gs, 1))
                dqkv[2, rows, lanes] = dot_nt(weigh3(g, 1), stack3(p, 1))

        for i in range(3):
            for h in range(2):
                put3(
                    rhs3.at[i], 0, pl.ds(h * half, half), dqkv[i, :, h * half : (h + 1) * half]
                )
        scaled = temporal_mix(lat_b) * twice(6)
        normal = lcol[...]
        first = jnp.sum(scaled, axis=0, keepdims=True) * (1.0 / C)
        second = jnp.sum(scaled * normal, axis=0, keepdims=True) * (1.0 / C)
        gcol[...] = gcol[...] + ln_rstd * (scaled - first - normal * second)
        for h in range(2):
            temporal(gcol[:, h * half : (h + 1) * half], h)
        scol[...] = temporal_mix(lte_b)
        pack_col(scol, GSP + r)
        a2a_send(GSP + r)
        pack_col(gcol, GHI + r)

    a2a_send(GHI)
    a2a_send(GHI + 1)

    @pl.loop(0, 2)
    def _(r):
        for h in range(2):
            put3(rhs1, 0, pl.ds(h * half, half), acol[r, :, h * half : (h + 1) * half])
        scol[...] = hcol[r] + dot(lout_f[...], rhs1[...])
        pack_col(scol, OUT + r)
        a2a_send(OUT + r)

    @pl.loop(0, 9)
    def _(t):
        prepare(wsp[8 - t], lsp.at[t])

    gs_up, gs_down = halo_copies(gs4, 2)

    def store_gs(r):
        def store(f, start, x):
            gs4[1 + r, f, pl.ds(start, 16), :] = x

        return store

    a2a_wait(GSP)
    unpack_frame(GSP, store_gs(0))
    gs_down.start()
    a2a_wait(GSP + 1)
    unpack_frame(GSP + 1, store_gs(1))
    gs_up.start()

    @pl.loop(1, 3)
    def _(r4):
        for f in range(2):
            shifted_rhs(r4, f, gs4[r4, f])

    gact[0] = conv(0, list(range(3, 9)), 3 * KDIM)
    gact[1] = conv(1, list(range(0, 6)), 3 * KDIM)

    def store_hid(r):
        def store(f, start, x):
            ghid[r, f, pl.ds(start, 16), :] = x

        return store

    def store_out(r):
        def store(f, start, x):
            output[f, r, pl.ds(start, 16), :] = x

        return store

    for r in range(2):
        a2a_wait(GHI + r)
        unpack_frame(GHI + r, store_hid(r))

    gs_up.wait_recv()
    gs_down.wait_recv()
    for r4 in (0, 3):
        for f in range(2):
            shifted_rhs(r4, f, jnp.where(inside(r4), gs4[r4, f], 0.0))
    gact[0] = gact[0] + conv(0, list(range(0, 3)), 0)
    gact[1] = gact[1] + conv(1, list(range(6, 9)), 9 * KDIM)

    parts = []
    for f in range(2):
        lanes = slice(f * LANES, (f + 1) * LANES)
        a = gact[0, :, lanes] * fac_s[1, f]
        b = gact[1, :, lanes] * fac_s[2, f]
        gact[0, :, lanes] = a
        gact[1, :, lanes] = b
        parts.append((a + b, a * hat_s[1, f] + b * hat_s[2, f]))
    pack_stats(1, [parts[0][0], parts[1][0], parts[0][1], parts[1][1]])
    send_stats(1)

    for r in range(2):
        a2a_wait(OUT + r)
        unpack_frame(OUT + r, store_out(r))

    spread(total_stats(1), 4)
    for r in range(2):
        for f in range(2):
            grad_latent[f, r] = ghid[r, f] + bcast[2 + f] * (
                gact[r, :, f * LANES : (f + 1) * LANES]
                - bcast[4 + f]
                - hat_s[1 + r, f] * bcast[6 + f]
            )

    for t in range(12):
        bytes_wait(sbuf.at[t, pl.ds(0, n_frame - 1)], ssem.at[t])
    for copy in (lat_up, lat_down, gs_up, gs_down):
        copy.wait_send()
    for which in range(2):
        bytes_wait(stat_r.at[which, pl.ds(0, n_row - 1)], stat_ss.at[which])


def per_device(
    n_frame,
    n_row,
    latent,
    cotangent,
    gn_gain,
    gn_bias,
    w_spatial,
    w_temporal,
    ln_gain,
    ln_bias,
    w_query,
    w_key,
    w_value,
    w_out,
):
    frames, rows, chans, cols = latent.shape
    vecs = jnp.concatenate(
        [jnp.stack([gn_gain, gn_bias, ln_gain, ln_bias]), jnp.zeros((4, chans), F32)]
    )
    anywhere = pl.BlockSpec(memory_space=pl.ANY)
    inside = pl.BlockSpec(memory_space=pltpu.VMEM)
    vm = pltpu.VMEM
    dma = pltpu.SemaphoreType.DMA
    return pl.pallas_call(
        functools.partial(kernel, n_frame, n_row),
        out_shape=(
            jax.ShapeDtypeStruct(latent.shape, F32),
            jax.ShapeDtypeStruct(latent.shape, F32),
        ),
        in_specs=[anywhere, anywhere, inside] + [anywhere] * 6,
        out_specs=(inside, inside),
        scratch_shapes=[
            vm((4, 2, C, LANES), F32),
            vm((2, 2, C, LANES), F32),
            vm((4, 2, C, LANES), F32),
            vm((4, 2, C, LANES), F32),
            vm((4, 2, C, LANES), F32),
            vm((2, 2, C, LANES), F32),
            vm((2, C, 256), F32),
            vm((9, C, C), F32),
            vm((3, C, C), F32),
            vm((4, C, C), F32),
            vm((9, C, KDIM), BF16),
            vm((3, C, KDIM), BF16),
            vm((3, C, KDIM), BF16),
            vm((3 * C, KDIM), BF16),
            vm((4, C, KDIM), BF16),
            vm((C, KDIM), BF16),
            vm((12 * KDIM, 256), BF16),
            vm((3, KDIM, 256), BF16),
            vm((KDIM, 256), BF16),
            vm((12, 8, QUARTER, LANES), F32),
            vm((12, 8, QUARTER, LANES), F32),
            vm((2, 8, LANES), F32),
            vm((2, n_row, 8, LANES), F32),
            vm((8, C, LANES), F32),
            vm((C, 256), F32),
            vm((C, 256), F32),
            vm((3 * C, 256), F32),
            vm((C, 256), F32),
            vm((2, C, 256), F32),
            vm((2, C, 256), F32),
            vm((3, C, 256), F32),
            dma((14,)),
            dma((12,)),
            dma((12,)),
            dma((4,)),
            dma((4,)),
            dma((2,)),
            dma((2,)),
        ],
        compiler_params=pltpu.CompilerParams(
            collective_id=0, has_side_effects=True, vmem_limit_bytes=62 * 1024 * 1024
        ),
        cost_estimate=pl.CostEstimate(flops=10**10, bytes_accessed=10**7, transcendentals=10**6),
    )(
        latent,
        cotangent,
        vecs,
        w_spatial.reshape(9, C, C),
        w_temporal,
        w_query,
        w_key,
        w_value,
        w_out,
    )


def solution(mesh):
    sizes = dict(mesh.shape)
    return jax.shard_map(
        functools.partial(per_device, sizes["frame"], sizes["row"]),
        mesh=mesh,
        in_specs=(P("frame", "row", None, None), P("frame", "row", None, None))
        + (P(),) * 10,
        out_specs=(P("frame", "row", None, None), P("frame", "row", None, None)),
        check_vma=False,
    )
```

profile of v0, /device:TPU:1, one launch (start us, length us, event | category | flops | bytes accessed | tf_op | source)
XLA Modules:
  0.0 110.6 jit_solution(6632556885381648720)
XLA Ops:
  0.6 0.7 stack.12
  1.3 0.7 stack.13
  2.0 0.7 stack.14
  2.7 0.7 stack.15
  3.4 0.6 concatenate.3.vecs
  4.0 102.6 %shard_map.131 = (f32[2,2,320,128]{3,2,1,0:T(8,128)}, f32[2,2,320,128]{3,2,1,0:T(8,128)}) custom-call(f32[2,2,320,128]{3,2,1,0:T(8,128)} %latent.1, f32[2,2,320,128]{3,2,1,0:T(8,128)} %cotangent.1, f32[8,320]{1,0:T(8,128)} %concatenate.3.vecs, f32[9,320,320]{2,1,0:T(8,128)} %bitcast.1, f32[3,320,320]{2,1,0:T(8,128)} %w_temporal.1, f32[320,320]{1,0:T(8,128)} %w_query.1, ...), custom_call_target="tpu_custom_call" | custom-call | flops 10000000000 | bytes 10000000 | tf_op jit(solution)/shard_map/pallas_call | solution.py:627
  106.6 2.0 %copy.16 = f32[2,2,320,128]{3,2,1,0:T(8,128)} copy(f32[2,2,320,128]{3,2,1,0:T(8,128)} %get-tuple-element.4) | data formatting | bytes 1310720
  108.6 2.0 %copy.17 = f32[2,2,320,128]{3,2,1,0:T(8,128)} copy(f32[2,2,320,128]{3,2,1,0:T(8,128)} %get-tuple-element.5) | data formatting | bytes 1310720
  (1 shorter events, 0.0 us)
where the time goes:
time: 111 us
  Pallas kernels  103 us (93%)
  local copies, waits for them, and re-layouts  7.29 us (7%)
    pallas_call x1, Pallas kernels, per_device(): pl.pallas_call(functools.partial(kernel, n_frame, n_row), out_shape=(jax....  103 us
    unnamed x2, local copies, waits for them, and re-layouts  3.93 us
    another operation x4, local copies, waits for them, and re-layouts, per_device(): jnp.stack([gn_gain, gn_bias, ln_gain, ln_bias])  2.73 us

commit v1 on v0

--- a/solution.py
+++ b/solution.py
@@ -97,15 +97,17 @@
     n_row,
     latent,
     cotangent,
-    vecs,
+    vec0,
+    vec1,
+    vec2,
+    vec3,
     w_spatial,
     w_temporal,
     w_query,
     w_key,
     w_value,
     w_out,
-    output,
-    grad_latent,
+    result,
     lat4,
     cot_own,
     gs4,
@@ -151,6 +153,7 @@
     has_low = ri > 0
     has_high = ri < n_row - 1
 
+    output, grad_latent = result.at[0], result.at[1]
     loads = []
     for r in range(2):
         for f in range(2):
@@ -204,7 +207,7 @@
         bytes_wait(rbuf.at[t, pl.ds(0, n_frame - 1)], rsem.at[t])
 
     def pack_frame(src, t):
-        @pl.loop(0, 5)
+        @pl.loop(0, 5, unroll=5)
         def _(i):
             xs = []
             for q in range(4):
@@ -214,7 +217,7 @@
                 sbuf[t, j, pl.ds(pl.multiple_of(i * 16, 16), 16), :] = x
 
     def unpack_frame(t, store):
-        @pl.loop(0, 5)
+        @pl.loop(0, 5, unroll=5)
         def _(i):
             at = pl.ds(pl.multiple_of(i * 16, 16), 16)
             ys = transpose_chunks([rbuf[t, j, at, :] for j in range(8)])
@@ -225,7 +228,7 @@
                 store(1, start, x1)
 
     def pack_col(src, t):
-        @pl.loop(0, 5)
+        @pl.loop(0, 5, unroll=5)
         def _(i):
             xs = []
             for q in range(4):
@@ -236,7 +239,7 @@
                 sbuf[t, s, pl.ds(pl.multiple_of(i * 16, 16), 16), :] = x
 
     def unpack_col(t, dst):
-        @pl.loop(0, 5)
+        @pl.loop(0, 5, unroll=5)
         def _(i):
             at = pl.ds(pl.multiple_of(i * 16, 16), 16)
             ys = transpose_chunks([rbuf[t, s, at, :] for s in range(8)])
@@ -343,7 +346,8 @@
     rhs1[pl.ds(960, 64), :] = jnp.zeros((64, 256), BF16)
 
     eye = (iota((C, C), 0) == iota((C, C), 1)).astype(F32)
-    cols = exact_nt(eye, vecs[...])
+    vecs = [v[...].reshape(1, C) for v in (vec0, vec1, vec2, vec3)] + [jnp.zeros((4, C), F32)]
+    cols = exact_nt(eye, jnp.concatenate(vecs, axis=0))
     for k in range(4):
         bcast[4 + k] = jnp.broadcast_to(cols[:, k : k + 1], (C, LANES))
 
@@ -414,7 +418,7 @@
         prepare(wte[2 - k], lte_b.at[k])
 
     half = LANES
-    same = (iota((half, half), 0) & 7) == (iota((half, half), 1) & 7)
+    same = (iota((half, 2 * half), 0) & 7) == (iota((half, 2 * half), 1) & 7)
     scale = HEAD_DIM ** (-0.5)
 
     def temporal(x, h):
@@ -431,18 +435,42 @@
     def twice(k):
         return jnp.concatenate([bcast[k], bcast[k]], axis=1)
 
-    def stack3(x, axis):
+    def stacked(x):
+        hi, lo = x
+        return jnp.concatenate([hi, lo, hi], axis=0)
+
+    def turned(x):
+        hi, lo = x
+        return jnp.concatenate([hi, hi, lo], axis=0).T
+
+    def diagonal(x):
+        return jnp.concatenate([x[:half, :half], x[half:, half:]], axis=1)
+
+    def both_ways(x):
         hi, lo = split(x)
-        return jnp.concatenate([hi, lo, hi], axis=axis)
-
-    def weigh3(x, axis):
-        hi, lo = split(x)
-        return jnp.concatenate([hi, hi, lo], axis=axis)
-
-    def turned(x):
-        hi = x.astype(BF16).astype(F32)
-        lo = x - hi
-        return jnp.concatenate([hi, hi, lo], axis=0).T.astype(BF16)
+        rows = jnp.concatenate([hi, lo], axis=0)
+        cols = [
+            jnp.concatenate([hi[:, h * half : (h + 1) * half], lo[:, h * half : (h + 1) * half]], axis=1)
+            for h in range(2)
+        ]
+        return rows, jnp.concatenate(cols, axis=0)
+
+    def pair(x):
+        hi, lo = x
+        zero = jnp.zeros((HEAD_DIM, half), BF16)
+        parts = []
+        for h in range(2):
+            a, b = hi[:, h * half : (h + 1) * half], lo[:, h * half : (h + 1) * half]
+            parts.append(jnp.concatenate([a, a], axis=1))
+            parts.append(jnp.concatenate([b, zero], axis=1))
+        return jnp.concatenate(parts, axis=0)
+
+    def folded(x):
+        d = HEAD_DIM
+        return jnp.concatenate(
+            [x[:d, :half] + x[d : 2 * d, :half], x[2 * d : 3 * d, half:] + x[3 * d :, half:]],
+            axis=1,
+        )
 
     @pl.loop(0, 2)
     def _(r):
@@ -471,23 +499,22 @@
         scol[...] = dot(lat_b[3], rhs1[...])
 
         for head in range(HEADS):
-            for h in range(2):
-                rows = slice(head * HEAD_DIM, (head + 1) * HEAD_DIM)
-                lanes = slice(h * half, (h + 1) * half)
-                q = qkv[rows, lanes]
-                k = qkv[C + head * HEAD_DIM : C + (head + 1) * HEAD_DIM, lanes]
-                v = qkv[2 * C + head * HEAD_DIM : 2 * C + (head + 1) * HEAD_DIM, lanes]
-                g = scol[rows, lanes]
-                scores = jnp.where(same, dot(turned(k), stack3(q, 0)) * scale, -1e30)
-                e = jnp.exp(scores - jnp.max(scores, axis=0, keepdims=True))
-                p = e * (1.0 / jnp.sum(e, axis=0, keepdims=True))
-                p3 = stack3(p, 0)
-                acol[r, rows, lanes] = dot(weigh3(v, 1), p3)
-                gp = dot(turned(v), stack3(g, 0))
-                gs = p * (gp - jnp.sum(p * gp, axis=0, keepdims=True)) * scale
-                dqkv[0, rows, lanes] = dot(weigh3(k, 1), stack3(gs, 0))
-                dqkv[1, rows, lanes] = dot_nt(weigh3(q, 1), stack3(gs, 1))
-                dqkv[2, rows, lanes] = dot_nt(weigh3(g, 1), stack3(p, 1))
+            rows = slice(head * HEAD_DIM, (head + 1) * HEAD_DIM)
+            q = split(qkv[rows, :])
+            k = split(qkv[C + head * HEAD_DIM : C + (head + 1) * HEAD_DIM, :])
+            v = split(qkv[2 * C + head * HEAD_DIM : 2 * C + (head + 1) * HEAD_DIM, :])
+            g = split(scol[rows, :])
+            scores = jnp.where(same, diagonal(dot(turned(k), stacked(q))) * scale, -1e30)
+            e = jnp.exp(scores - jnp.max(scores, axis=0, keepdims=True))
+            p = e * (1.0 / jnp.sum(e, axis=0, keepdims=True))
+            gp = diagonal(dot(turned(v), stacked(g)))
+            gs = p * (gp - jnp.sum(p * gp, axis=0, keepdims=True)) * scale
+            p_rows, p_cols = both_ways(p)
+            s_rows, s_cols = both_ways(gs)
+            acol[r, rows, :] = folded(dot(pair(v), p_rows))
+            dqkv[0, rows, :] = folded(dot(pair(k), s_rows))
+            dqkv[1, rows, :] = folded(dot_nt(pair(q), s_cols))
+            dqkv[2, rows, :] = folded(dot_nt(pair(g), p_cols))
 
         for i in range(3):
             for h in range(2):
@@ -505,9 +532,7 @@
         pack_col(scol, GSP + r)
         a2a_send(GSP + r)
         pack_col(gcol, GHI + r)
-
-    a2a_send(GHI)
-    a2a_send(GHI + 1)
+        a2a_send(GHI + r)
 
     @pl.loop(0, 2)
     def _(r):
@@ -617,21 +642,15 @@
     w_out,
 ):
     frames, rows, chans, cols = latent.shape
-    vecs = jnp.concatenate(
-        [jnp.stack([gn_gain, gn_bias, ln_gain, ln_bias]), jnp.zeros((4, chans), F32)]
-    )
     anywhere = pl.BlockSpec(memory_space=pl.ANY)
     inside = pl.BlockSpec(memory_space=pltpu.VMEM)
     vm = pltpu.VMEM
     dma = pltpu.SemaphoreType.DMA
-    return pl.pallas_call(
+    result = pl.pallas_call(
         functools.partial(kernel, n_frame, n_row),
-        out_shape=(
-            jax.ShapeDtypeStruct(latent.shape, F32),
-            jax.ShapeDtypeStruct(latent.shape, F32),
-        ),
-        in_specs=[anywhere, anywhere, inside] + [anywhere] * 6,
-        out_specs=(inside, inside),
+        out_shape=jax.ShapeDtypeStruct((2,) + latent.shape, F32),
+        in_specs=[anywhere, anywhere] + [inside] * 4 + [anywhere] * 6,
+        out_specs=inside,
         scratch_shapes=[
             vm((4, 2, C, LANES), F32),
             vm((2, 2, C, LANES), F32),
@@ -679,7 +698,10 @@
     )(
         latent,
         cotangent,
-        vecs,
+        gn_gain,
+        gn_bias,
+        ln_gain,
+        ln_bias,
         w_spatial.reshape(9, C, C),
         w_temporal,
         w_query,
@@ -687,6 +709,7 @@
         w_value,
         w_out,
     )
+    return result[0], result[1]
 
 
 def solution(mesh):

time: 111 us -> 80.9 us (0.73)
  Pallas kernels: 103 us -> 77.7 us
  local copies, waits for them, and re-layouts: 7.29 us -> 2.43 us
    pallas_call x1, Pallas kernels: 103 us -> 77.7 us  [per_device(): pl.pallas_call(functools.partial(kernel, n_frame, n_row), out_shape=jax.S...]
    unnamed x2 -> x0, local copies, waits for them, and re-layouts: 3.93 us -> none
    another operation x4 -> x0, local copies, waits for them, and re-layouts: 2.73 us -> none  [per_device(): jnp.stack([gn_gain, gn_bias, ln_gain, ln_bias])]
    squeeze x0 -> x1, local copies, waits for them, and re-layouts: none -> 2.43 us  [per_device(): return (result[0], result[1])]
where the time goes in v1:
time: 80.9 us; the launch traced here: 80.7 us
  Pallas kernels  77.7 us (96%)
  local copies, waits for them, and re-layouts  2.43 us (3%)
    pallas_call x1, Pallas kernels, per_device(): pl.pallas_call(functools.partial(kernel, n_frame, n_row), out_shape=jax.S...  77.7 us
    squeeze x1, local copies, waits for them, and re-layouts, per_device(): return (result[0], result[1])  2.43 us

profile of v1, /device:TPU:1, one launch (start us, length us, event | category | flops | bytes accessed | tf_op | source)
XLA Modules:
  0.0 80.7 jit_solution(10486452381918947404)
XLA Ops:
  0.6 77.7 %shard_map.131 = f32[2,2,2,320,128]{4,3,2,1,0:T(8,128)} custom-call(f32[2,2,320,128]{3,2,1,0:T(8,128)} %latent.1, f32[2,2,320,128]{3,2,1,0:T(8,128)} %cotangent.1, f32[320]{0:T(512)} %vec0.1, f32[320]{0:T(512)} %vec1.1, f32[320]{0:T(512)} %vec2.1, f32[320]{0:T(512)} %vec3.1, f32[9,320,320]{2,1,0:T(8,128)} %bitcast.5, f32[3,320,320]{2,1,0:T(8,128)} %w_temporal.1, ...), custom_call_target="tpu_custom_call" | custom-call | flops 10000000000 | bytes 10000000 | tf_op jit(solution)/shard_map/pallas_call | solution.py:649
  78.3 2.4 %slice_bitcast_fusion = (f32[2,2,320,128]{3,2,1,0:T(8,128)}, f32[2,2,320,128]{3,2,1,0:T(8,128)}) fusion(f32[2,2,2,320,128]{4,3,2,1,0:T(8,128)} %shard_map.131), kind=kLoop, calls=%fused_computation | loop fusion | bytes 2621440 | tf_op jit(solution)/shard_map/squeeze | solution.py:712

commit v2 on v1

--- a/solution.py
+++ b/solution.py
@@ -108,6 +108,7 @@
     w_value,
     w_out,
     result,
+    res_v,
     lat4,
     cot_own,
     gs4,
@@ -115,6 +116,7 @@
     fac_s,
     ghid,
     gact,
+    share,
     wsp,
     wte,
     wat,
@@ -140,6 +142,7 @@
     hcol,
     dqkv,
     load_sem,
+    store_sem,
     ssem,
     rsem,
     halo_s,
@@ -153,7 +156,6 @@
     has_low = ri > 0
     has_high = ri < n_row - 1
 
-    output, grad_latent = result.at[0], result.at[1]
     loads = []
     for r in range(2):
         for f in range(2):
@@ -168,9 +170,15 @@
     copies = [
         pltpu.make_async_copy(src, dst, load_sem.at[i]) for i, (src, dst) in enumerate(loads)
     ]
-    for c in copies:
+    for c in copies[:8]:
         c.start()
 
+    stores = [
+        pltpu.make_async_copy(res_v.at[i, f, r], result.at[i, f, r], store_sem.at[4 * i + 2 * r + f])
+        for i in range(2)
+        for r in range(2)
+        for f in range(2)
+    ]
     barrier = pltpu.get_barrier_semaphore()
 
     @pl.loop(1, n_row)
@@ -249,8 +257,9 @@
                     dst[pl.ds(start, 16), h * LANES : (h + 1) * LANES] = ys[2 * q + h]
 
     chan = iota((C, LANES), 0)
-    group = iota((C, LANES), 1)
-    member = ((chan >= group * PER_GROUP) & (chan < group * PER_GROUP + PER_GROUP)).astype(F32)
+    first = (iota((C, LANES), 1) & (GROUPS - 1)) * PER_GROUP
+    member = ((chan >= first) & (chan < first + PER_GROUP)).astype(F32)
+    own_chunk = (iota((8, LANES), 1) // GROUPS) == iota((8, LANES), 0)
 
     def pack_stats(which, parts):
         total = jnp.zeros((8, C), F32)
@@ -258,27 +267,32 @@
         for k, part in enumerate(parts):
             total = total + exact_nt((at == k).astype(F32), part)
         tile = jnp.dot(total, member, precision=HIGHEST, preferred_element_type=F32)
-        stat_s[which] = tile
-        stat_r[which, ri] = tile
+        row = jnp.sum(jnp.where(own_chunk, tile, 0.0), axis=0, keepdims=True)
+        stat_s[which] = jnp.broadcast_to(row, (8, LANES))
+        stat_r[which, ri, pl.ds(0, 1), :] = row
 
     def send_stats(which):
         @pl.loop(1, n_row)
         def _(k):
             pltpu.make_async_remote_copy(
-                src_ref=stat_s.at[which],
-                dst_ref=stat_r.at[which, ri],
+                src_ref=stat_s.at[which, pl.ds(0, 1)],
+                dst_ref=stat_r.at[which, ri, pl.ds(0, 1)],
                 send_sem=stat_ss.at[which],
                 recv_sem=stat_rs.at[which],
                 device_id={"row": lax.rem(ri + k, n_row)},
                 device_id_type=MESH,
             ).start()
 
+    def stats_wait(which, sems):
+        bytes_wait(stat_r.at[which, pl.ds(0, n_row - 1), pl.ds(0, 1)], sems.at[which])
+
     def total_stats(which):
-        bytes_wait(stat_r.at[which, pl.ds(0, n_row - 1)], stat_rs.at[which])
-        return jnp.sum(stat_r[which], axis=0) * (1.0 / members)
-
-    def spread(rows, at):
-        cols = exact_nt(member, rows)
+        stats_wait(which, stat_rs)
+        total = jnp.sum(stat_r[which, :, 0:1, :], axis=0) * (1.0 / members)
+        return jnp.broadcast_to(total, (8, LANES))
+
+    def spread(row, at):
+        cols = exact_nt(member, jnp.where(own_chunk, row, 0.0))
         for k in range(4):
             bcast[at + k] = jnp.broadcast_to(cols[:, k : k + 1], (C, LANES))
 
@@ -301,8 +315,13 @@
         )
         return up, down
 
+    def on(condition, action):
+        pl.when(condition)(lambda: action())
+
     for c in copies[:4]:
         c.wait()
+    for c in copies[8:]:
+        c.start()
     parts = []
     for f in range(2):
         a, b = lat4[1, f], lat4[2, f]
@@ -311,20 +330,26 @@
         a, b = lat4[1, f], lat4[2, f]
         parts.append(a * a + b * b)
     pack_stats(0, parts)
-    for r in range(2):
+
+    def pack_latent(r):
         pack_frame(lambda f, start: lat4[1 + r, f, pl.ds(start, 16), :], LAT + r)
+
+    def pack_cotangent(r):
+        pack_frame(lambda f, start: cot_own[r, f, pl.ds(start, 16), :], COT + r)
+
+    pack_latent(0)
+    pl.semaphore_wait(barrier, n_row - 1 + n_frame - 1)
+    lat_up, lat_down = halo_copies(lat4, 0)
+    on(has_high, lat_up.start)
+    on(has_low, lat_down.start)
+    a2a_send(LAT)
+    send_stats(0)
+    pack_latent(1)
+    a2a_send(LAT + 1)
     for c in copies[4:8]:
         c.wait()
-    for r in range(2):
-        pack_frame(lambda f, start: cot_own[r, f, pl.ds(start, 16), :], COT + r)
-
-    pl.semaphore_wait(barrier, n_row - 1 + n_frame - 1)
-    send_stats(0)
-    lat_up, lat_down = halo_copies(lat4, 0)
-    lat_up.start()
-    lat_down.start()
-    a2a_send(LAT)
-    a2a_send(COT)
+    pack_cotangent(0)
+    pack_cotangent(1)
 
     for c in copies[8:]:
         c.wait()
@@ -352,13 +377,11 @@
         bcast[4 + k] = jnp.broadcast_to(cols[:, k : k + 1], (C, LANES))
 
     mean2 = total_stats(0)
-    at8 = iota((8, LANES), 0)
-    var = pltpu.roll(mean2, 6, 0) - mean2 * mean2
-    rstd = lax.rsqrt(jnp.where(at8 < 2, var, 1.0) + EPSILON)
-    spread(jnp.where(at8 < 2, mean2, pltpu.roll(rstd, 2, 0)), 0)
-
-    lat_up.wait_recv()
-    lat_down.wait_recv()
+    a2a_send(COT)
+    is_mean = iota((8, LANES), 1) < 2 * GROUPS
+    var = roll(mean2, 2 * GROUPS) - mean2 * mean2
+    rstd = lax.rsqrt(jnp.where(is_mean, var, 1.0) + EPSILON)
+    spread(jnp.where(is_mean, mean2, roll(rstd, 2 * GROUPS)), 0)
 
     lane = iota((C, LANES), 1)
 
@@ -376,18 +399,17 @@
     def inside(r4):
         return ((r4 > 0) | has_low) & ((r4 < 3) | has_high)
 
-    @pl.loop(0, 4)
-    def _(r4):
+    def forward_rhs(r4):
         for f in range(2):
             hat = (lat4[r4, f] - bcast[f]) * bcast[2 + f]
             shifted = hat * bcast[4] + bcast[5]
             sigma = 1.0 / (1.0 + jnp.exp(-shifted))
-            act = shifted * sigma
-            hat_s[r4, f] = hat
-            fac_s[r4, f] = sigma * (1.0 + shifted * (1.0 - sigma)) * bcast[4]
-            shifted_rhs(r4, f, jnp.where(inside(r4), act, 0.0))
-
-    def conv(rows, taps, base):
+            slope = sigma * (1.0 + shifted * (1.0 - sigma)) * bcast[4]
+            hat_s[r4, f] = jnp.where(inside(r4), hat, 0.0)
+            fac_s[r4, f] = jnp.where(inside(r4), slope, 0.0)
+            shifted_rhs(r4, f, jnp.where(inside(r4), shifted * sigma, 0.0))
+
+    def conv(taps, base):
         total = None
         for t in taps:
             start = pl.multiple_of(base + (t - taps[0]) * KDIM, KDIM)
@@ -395,19 +417,24 @@
             total = term if total is None else total + term
         return total
 
-    @pl.loop(0, 2)
-    def _(r):
-        scol[...] = conv(r, list(range(9)), r * (3 * KDIM))
+    def send_spatial(r):
         pack_frame(
             lambda f, start: scol[pl.ds(start, 16), f * LANES : (f + 1) * LANES], SPA + r
         )
         a2a_send(SPA + r)
 
-        @pl.when(r == 0)
-        def _():
-            a2a_send(LAT + 1)
-
-    a2a_send(COT + 1)
+    forward_rhs(1)
+    forward_rhs(2)
+    own = conv(list(range(3, 9)), 3 * KDIM)
+    on(has_low, lat_up.wait_recv)
+    forward_rhs(0)
+    scol[...] = own + conv(list(range(0, 3)), 0)
+    send_spatial(0)
+    own = conv(list(range(0, 6)), 3 * KDIM)
+    on(has_high, lat_down.wait_recv)
+    forward_rhs(3)
+    scol[...] = own + conv(list(range(6, 9)), 9 * KDIM)
+    send_spatial(1)
 
     for i in range(3):
         prepare(wat[i].T, lqkv.at[pl.ds(i * C, C)])
@@ -477,6 +504,11 @@
         a2a_wait(LAT + r)
         unpack_col(LAT + r, lcol)
         a2a_wait(SPA + r)
+
+        @pl.when(r == 0)
+        def _():
+            a2a_send(COT + 1)
+
         unpack_col(SPA + r, scol)
         for h in range(2):
             temporal(scol[:, h * half : (h + 1) * half], h)
@@ -532,7 +564,35 @@
         pack_col(scol, GSP + r)
         a2a_send(GSP + r)
         pack_col(gcol, GHI + r)
-        a2a_send(GHI + r)
+
+        @pl.when(r == 0)
+        def _():
+            a2a_send(GHI)
+
+
+    gs_up, gs_down = halo_copies(gs4, 2)
+
+    def store_gs(r):
+        def store(f, start, x):
+            gs4[1 + r, f, pl.ds(start, 16), :] = x
+
+        return store
+
+    def store_hid(r):
+        def store(f, start, x):
+            ghid[r, f, pl.ds(start, 16), :] = x
+
+        return store
+
+    def store_out(r):
+        def store(f, start, x):
+            res_v[0, f, r, pl.ds(start, 16), :] = x
+
+        return store
+
+    a2a_wait(GSP)
+    unpack_frame(GSP, store_gs(0))
+    on(has_low, gs_down.start)
 
     @pl.loop(0, 2)
     def _(r):
@@ -540,89 +600,78 @@
             put3(rhs1, 0, pl.ds(h * half, half), acol[r, :, h * half : (h + 1) * half])
         scol[...] = hcol[r] + dot(lout_f[...], rhs1[...])
         pack_col(scol, OUT + r)
-        a2a_send(OUT + r)
+
+    a2a_send(GHI + 1)
 
     @pl.loop(0, 9)
     def _(t):
         prepare(wsp[8 - t], lsp.at[t])
 
-    gs_up, gs_down = halo_copies(gs4, 2)
-
-    def store_gs(r):
-        def store(f, start, x):
-            gs4[1 + r, f, pl.ds(start, 16), :] = x
-
-        return store
-
-    a2a_wait(GSP)
-    unpack_frame(GSP, store_gs(0))
-    gs_down.start()
     a2a_wait(GSP + 1)
     unpack_frame(GSP + 1, store_gs(1))
-    gs_up.start()
-
-    @pl.loop(1, 3)
-    def _(r4):
+    on(has_high, gs_up.start)
+    a2a_send(OUT)
+    a2a_send(OUT + 1)
+
+    def back_rhs(r4):
         for f in range(2):
-            shifted_rhs(r4, f, gs4[r4, f])
-
-    gact[0] = conv(0, list(range(3, 9)), 3 * KDIM)
-    gact[1] = conv(1, list(range(0, 6)), 3 * KDIM)
-
-    def store_hid(r):
-        def store(f, start, x):
-            ghid[r, f, pl.ds(start, 16), :] = x
-
-        return store
-
-    def store_out(r):
-        def store(f, start, x):
-            output[f, r, pl.ds(start, 16), :] = x
-
-        return store
+            shifted_rhs(r4, f, jnp.where(inside(r4), gs4[r4, f], 0.0))
+
+    for r4 in (1, 2):
+        back_rhs(r4)
+    gact[0] = conv(list(range(3, 9)), 3 * KDIM)
+    gact[1] = conv(list(range(0, 6)), 3 * KDIM)
+    share[0] = conv(list(range(6, 9)), 3 * KDIM)
+    share[1] = conv(list(range(0, 3)), 6 * KDIM)
+    sums, crosses = [], []
+    for f in range(2):
+        lanes = slice(f * LANES, (f + 1) * LANES)
+        first = second = None
+        for r4, g in ((0, share.at[0]), (1, gact.at[0]), (2, gact.at[1]), (3, share.at[1])):
+            a = g[:, lanes] * fac_s[r4, f]
+            b = a * hat_s[r4, f]
+            first = a if first is None else first + a
+            second = b if second is None else second + b
+        sums.append(first)
+        crosses.append(second)
+    pack_stats(1, sums + crosses)
+    send_stats(1)
+
+    on(has_high, gs_down.wait_recv)
+    back_rhs(3)
+    gact[1] = gact[1] + conv(list(range(6, 9)), 9 * KDIM)
+    on(has_low, gs_up.wait_recv)
+    back_rhs(0)
+    gact[0] = gact[0] + conv(list(range(0, 3)), 0)
 
     for r in range(2):
         a2a_wait(GHI + r)
         unpack_frame(GHI + r, store_hid(r))
-
-    gs_up.wait_recv()
-    gs_down.wait_recv()
-    for r4 in (0, 3):
-        for f in range(2):
-            shifted_rhs(r4, f, jnp.where(inside(r4), gs4[r4, f], 0.0))
-    gact[0] = gact[0] + conv(0, list(range(0, 3)), 0)
-    gact[1] = gact[1] + conv(1, list(range(6, 9)), 9 * KDIM)
-
-    parts = []
-    for f in range(2):
-        lanes = slice(f * LANES, (f + 1) * LANES)
-        a = gact[0, :, lanes] * fac_s[1, f]
-        b = gact[1, :, lanes] * fac_s[2, f]
-        gact[0, :, lanes] = a
-        gact[1, :, lanes] = b
-        parts.append((a + b, a * hat_s[1, f] + b * hat_s[2, f]))
-    pack_stats(1, [parts[0][0], parts[1][0], parts[0][1], parts[1][1]])
-    send_stats(1)
-
     for r in range(2):
         a2a_wait(OUT + r)
         unpack_frame(OUT + r, store_out(r))
+        for f in range(2):
+            stores[2 * r + f].start()
 
     spread(total_stats(1), 4)
     for r in range(2):
         for f in range(2):
-            grad_latent[f, r] = ghid[r, f] + bcast[2 + f] * (
-                gact[r, :, f * LANES : (f + 1) * LANES]
+            res_v[1, f, r] = ghid[r, f] + bcast[2 + f] * (
+                gact[r, :, f * LANES : (f + 1) * LANES] * fac_s[1 + r, f]
                 - bcast[4 + f]
                 - hat_s[1 + r, f] * bcast[6 + f]
             )
-
+            stores[4 + 2 * r + f].start()
+
+    for c in stores:
+        c.wait()
     for t in range(12):
         bytes_wait(sbuf.at[t, pl.ds(0, n_frame - 1)], ssem.at[t])
-    for copy in (lat_up, lat_down, gs_up, gs_down):
-        copy.wait_send()
+    for up, down in ((lat_up, lat_down), (gs_up, gs_down)):
+        on(has_high, up.wait_send)
+        on(has_low, down.wait_send)
     for which in range(2):
-        bytes_wait(stat_r.at[which, pl.ds(0, n_row - 1)], stat_ss.at[which])
+        stats_wait(which, stat_ss)
 
 
 def per_device(
@@ -650,14 +699,16 @@
         functools.partial(kernel, n_frame, n_row),
         out_shape=jax.ShapeDtypeStruct((2,) + latent.shape, F32),
         in_specs=[anywhere, anywhere] + [inside] * 4 + [anywhere] * 6,
-        out_specs=inside,
+        out_specs=anywhere,
         scratch_shapes=[
+            vm((2, 2, 2, C, LANES), F32),
             vm((4, 2, C, LANES), F32),
             vm((2, 2, C, LANES), F32),
             vm((4, 2, C, LANES), F32),
             vm((4, 2, C, LANES), F32),
             vm((4, 2, C, LANES), F32),
             vm((2, 2, C, LANES), F32),
+            vm((2, C, 256), F32),
             vm((2, C, 256), F32),
             vm((9, C, C), F32),
             vm((3, C, C), F32),
@@ -684,6 +735,7 @@
             vm((2, C, 256), F32),
             vm((3, C, 256), F32),
             dma((14,)),
+            dma((8,)),
             dma((12,)),
             dma((12,)),
             dma((4,)),

time: 80.9 us -> 78.5 us (0.970)
  Pallas kernels: 77.7 us -> 75.3 us
    pallas_call x1, Pallas kernels: 77.7 us -> 75.3 us  [per_device(): pl.pallas_call(functools.partial(kernel, n_frame, n_row), out_shape=jax.S...]
where the time goes in v2:
time: 78.5 us; the launch traced here: 78.4 us
  Pallas kernels  75.3 us (96%)
  local copies, waits for them, and re-layouts  2.43 us (3%)
    pallas_call x1, Pallas kernels, per_device(): pl.pallas_call(functools.partial(kernel, n_frame, n_row), out_shape=jax.S...  75.3 us
    squeeze x1, local copies, waits for them, and re-layouts, per_device(): return (result[0], result[1])  2.43 us

profile of v2, /device:TPU:1, one launch (start us, length us, event | category | flops | bytes accessed | tf_op | source)
XLA Modules:
  0.0 78.4 jit_solution(3484613686766866028)
XLA Ops:
  0.6 75.3 %shard_map.131 = f32[2,2,2,320,128]{4,3,2,1,0:T(8,128)} custom-call(f32[2,2,320,128]{3,2,1,0:T(8,128)} %latent.1, f32[2,2,320,128]{3,2,1,0:T(8,128)} %cotangent.1, f32[320]{0:T(512)} %vec0.1, f32[320]{0:T(512)} %vec1.1, f32[320]{0:T(512)} %vec2.1, f32[320]{0:T(512)} %vec3.1, f32[9,320,320]{2,1,0:T(8,128)} %bitcast.5, f32[3,320,320]{2,1,0:T(8,128)} %w_temporal.1, ...), custom_call_target="tpu_custom_call" | custom-call | flops 10000000000 | bytes 10000000 | tf_op jit(solution)/shard_map/pallas_call | solution.py:698
  76.0 2.4 %slice_bitcast_fusion = (f32[2,2,320,128]{3,2,1,0:T(8,128)}, f32[2,2,320,128]{3,2,1,0:T(8,128)}) fusion(f32[2,2,2,320,128]{4,3,2,1,0:T(8,128)} %shard_map.131), kind=kLoop, calls=%fused_computation | loop fusion | bytes 2621440 | tf_op jit(solution)/shard_map/squeeze | solution.py:764

commit v3 on v2

--- a/solution.py
+++ b/solution.py
@@ -193,10 +193,12 @@
             barrier, inc=1, device_id={"frame": lax.rem(fi + k, n_frame)}, device_id_type=MESH
         )
 
+    ring = 4 if n_frame % 4 == 0 else n_frame
+
     def a2a_send(t):
         @pl.loop(1, n_frame)
         def _(k):
-            dest = lax.rem(fi + k, n_frame)
+            dest = lax.rem(fi // ring + k // ring, n_frame // ring) * ring + lax.rem(fi + k, ring)
             pltpu.make_async_remote_copy(
                 src_ref=sbuf.at[t, dest],
                 dst_ref=rbuf.at[t, fi],
@@ -342,8 +344,8 @@
     lat_up, lat_down = halo_copies(lat4, 0)
     on(has_high, lat_up.start)
     on(has_low, lat_down.start)
+    send_stats(0)
     a2a_send(LAT)
-    send_stats(0)
     pack_latent(1)
     a2a_send(LAT + 1)
     for c in copies[4:8]:
@@ -600,6 +602,7 @@
             put3(rhs1, 0, pl.ds(h * half, half), acol[r, :, h * half : (h + 1) * half])
         scol[...] = hcol[r] + dot(lout_f[...], rhs1[...])
         pack_col(scol, OUT + r)
+        a2a_send(OUT + r)
 
     a2a_send(GHI + 1)
 
@@ -610,8 +613,6 @@
     a2a_wait(GSP + 1)
     unpack_frame(GSP + 1, store_gs(1))
     on(has_high, gs_up.start)
-    a2a_send(OUT)
-    a2a_send(OUT + 1)
 
     def back_rhs(r4):
         for f in range(2):

time: 78.5 us -> 77.4 us (0.986)
  Pallas kernels: 75.3 us -> 74.2 us
    pallas_call x1, Pallas kernels: 75.3 us -> 74.2 us  [per_device(): pl.pallas_call(functools.partial(kernel, n_frame, n_row), out_shape=jax.S...]
where the time goes in v3:
time: 77.4 us; the launch traced here: 77.3 us
  Pallas kernels  74.2 us (96%)
  local copies, waits for them, and re-layouts  2.43 us (3%)
    pallas_call x1, Pallas kernels, per_device(): pl.pallas_call(functools.partial(kernel, n_frame, n_row), out_shape=jax.S...  74.2 us
    squeeze x1, local copies, waits for them, and re-layouts, per_device(): return (result[0], result[1])  2.43 us

profile of v3, /device:TPU:1, one launch (start us, length us, event | category | flops | bytes accessed | tf_op | source)
XLA Modules:
  0.0 77.3 jit_solution(16959004282139411712)
XLA Ops:
  0.6 74.2 %shard_map.131 = f32[2,2,2,320,128]{4,3,2,1,0:T(8,128)} custom-call(f32[2,2,320,128]{3,2,1,0:T(8,128)} %latent.1, f32[2,2,320,128]{3,2,1,0:T(8,128)} %cotangent.1, f32[320]{0:T(512)} %vec0.1, f32[320]{0:T(512)} %vec1.1, f32[320]{0:T(512)} %vec2.1, f32[320]{0:T(512)} %vec3.1, f32[9,320,320]{2,1,0:T(8,128)} %bitcast.5, f32[3,320,320]{2,1,0:T(8,128)} %w_temporal.1, ...), custom_call_target="tpu_custom_call" | custom-call | flops 10000000000 | bytes 10000000 | tf_op jit(solution)/shard_map/pallas_call | solution.py:699
  74.9 2.4 %slice_bitcast_fusion = (f32[2,2,320,128]{3,2,1,0:T(8,128)}, f32[2,2,320,128]{3,2,1,0:T(8,128)}) fusion(f32[2,2,2,320,128]{4,3,2,1,0:T(8,128)} %shard_map.131), kind=kLoop, calls=%fused_computation | loop fusion | bytes 2621440 | tf_op jit(solution)/shard_map/squeeze | solution.py:765
